TPU v7x, 256 devices: a whole 4x4x8 slice. The times are simulated.
256 devices in a mesh: seg: 16 (over z, core), bond: 16 (over x, y).
Axes of the slice: x: 4, y: 4, z: 8, core: 2. Of those that a mesh axis runs over, the one named last changes fastest.
Arguments:
- left_env: bfloat16 [16, 1024, 6, 1024], P('seg', 'bond'), may hold values from -0.1875 to 0.1875
- prev_left: bfloat16 [16, 1024, 1024], P('seg'), may hold values from -0.25 to 1.25
- cur_site: bfloat16 [16, 1024, 4, 1024], P('seg', 'bond'), may hold values from -6 to 6
- prev_site: bfloat16 [16, 1024, 4, 1024], P('seg', None, None, 'bond'), may hold values from -6 to 6
- hamiltonian: bfloat16 [16, 6, 6, 4, 4], P('seg'), may hold values from -1.25 to 1.25
- right_env: bfloat16 [16, 1024, 6, 1024], P('seg', 'bond'), may hold values from -0.078125 to 0.078125
- prev_right: bfloat16 [16, 1024, 1024], P('seg'), may hold values from -0.25 to 1.25
Outputs:
- new_site: bfloat16 [16, 1024, 4, 1024], P('seg', 'bond')
- center: float32 [16, 1024, 1024], P('seg', 'bond')
All inputs are finite; a program needn't handle non-finite values.
Results may differ from a plain program's by a relative error of at most 0.0054.
Values may be sent and summed in bfloat16 or wider, within the bound.
No kernel may reach another device: no remote copies, remote signals or barrier semaphores. Data moves between devices by JAX's collectives and lax.ppermute only.
A program may use at most 128 MiB of HBM per device.

v0:
```python
import math
import jax
import jax.numpy as jnp
from jax import lax
from jax.sharding import PartitionSpec as P

PHYS = 4
MPOB = 6


def shifted(block, axis, distance):
    devices = range(lax.axis_size(axis))
    route = [((i - distance) % len(devices), i) for i in devices]
    return lax.ppermute(block, axis, route)


def shards(left_env, prev_left, cur_site, prev_site, hamiltonian, right_env, prev_right):
    left_now, prev_now = shifted((left_env[0], prev_left[0]), "seg", 1)
    own_rows = left_now.shape[0]
    bond_width = left_now.shape[2]
    coupling = hamiltonian[0].astype(jnp.float32)
    current = lax.all_gather(cur_site[0], "bond", axis=0, tiled=True)
    projected = jnp.dot(
        left_now.reshape(own_rows * MPOB, bond_width),
        current.reshape(bond_width, PHYS * bond_width),
        preferred_element_type=jnp.float32,
    ).reshape(own_rows, MPOB, PHYS, bond_width)
    mixture = jnp.einsum(
        "autc,uvst->asvc", projected, coupling, precision=lax.Precision.HIGHEST
    ).astype(jnp.bfloat16)
    applied = jnp.einsum(
        "asvc,cvy->asy",
        mixture,
        lax.all_gather(right_env[0], "bond", axis=0, tiled=True),
        preferred_element_type=jnp.float32,
    )
    previous = lax.all_gather(prev_site[0], "bond", axis=2, tiled=True)
    own_left = lax.dynamic_slice_in_dim(prev_now, lax.axis_index("bond") * own_rows, own_rows, 0)
    partial_value = jnp.einsum(
        "ab,bsc->asc", own_left, previous, preferred_element_type=jnp.float32
    ).astype(jnp.bfloat16)
    second = jnp.einsum(
        "asc,cy->asy", partial_value, prev_right[0], preferred_element_type=jnp.float32
    )
    target = (2.0 * applied - second).reshape(own_rows * PHYS, bond_width)
    local_correlation = jnp.dot(
        target.T, target, precision=lax.Precision.HIGHEST, preferred_element_type=jnp.float32
    )
    correlation = lax.psum(local_correlation, "bond")
    triangle = jnp.linalg.cholesky(correlation)
    solved = jax.scipy.linalg.solve_triangular(triangle, target.T, lower=True)
    norming = math.sqrt(bond_width * PHYS)
    new_site = (solved.T * norming).astype(jnp.bfloat16).reshape(1, own_rows, PHYS, bond_width)
    offset = lax.axis_index("bond") * own_rows
    center = lax.dynamic_slice_in_dim(triangle.T, offset, own_rows, 0) / norming
    return (new_site, center[None])


def solution(mesh):
    return jax.shard_map(
        shards,
        mesh=mesh,
        in_specs=(
            P("seg", "bond", None, None),
            P("seg", None, None),
            P("seg", "bond", None, None),
            P("seg", None, None, "bond"),
            P("seg", None, None, None, None),
            P("seg", "bond", None, None),
            P("seg", None, None),
        ),
        out_specs=(P("seg", "bond", None, None), P("seg", "bond", None)),
        check_vma=False,
    )
```

profile of v0, /device:TPU:1, one launch (start us, length us, event | category | flops | bytes accessed | tf_op | source)
XLA Modules:
  0.0 756.7 jit_solution(14787921494383537855)
XLA Ops:
  8.0 2.2 copy.56
  11.0 3.0 collective-permute-start
  14.1 75.9 %all-gather.7.cloned.1.call-done = bf16[1,1024,4,1024]{3,2,0,1:T(4,128)(2,1)} async-done(((bf16[1,64,4,1024]{3,2,0,1:T(4,128)(2,1)}), bf16[1,1024,4,1024]{3,2,0,1:T(4,128)(2,1)}) %all-gather.7.cloned.1.call-update) | async-done | bytes 8388624 | tf_op jit(solution)/shard_map/all_gather | solution.py:22
  90.0 13.8 %copy.82 = bf16[1,1024,4,1024]{1,3,2,0:T(8,128)(2,1)} copy(bf16[1,1024,4,1024]{3,2,0,1:T(4,128)(2,1)} %all-gather.7.cloned.1.call-done) | data formatting | bytes 16777216 | tf_op jit(solution)/shard_map/reshape | solution.py:25
  103.9 64.7 %all-gather.11.cloned.1.call-done = bf16[1,1024,4,1024]{1,2,0,3:T(4,128)(2,1)} async-done(((bf16[1,1024,4,64]{1,2,0,3:T(4,128)(2,1)}), bf16[1,1024,4,1024]{1,2,0,3:T(4,128)(2,1)}) %all-gather.11.cloned.1.call-update) | async-done | bytes 8388624 | tf_op jit(solution)/shard_map/all_gather | solution.py:37
  168.6 13.7 %copy.57 = bf16[1,1024,4,1024]{3,1,2,0:T(8,128)(2,1)} copy(bf16[1,1024,4,1024]{1,2,0,3:T(4,128)(2,1)} %all-gather.11.cloned.1.call-done) | data formatting | bytes 16777216 | tf_op jit(solution)/shard_map/all_gather | solution.py:37
  182.3 6.3 fusion.14
  188.6 11.5 %fusion.8 = bf16[64,4,6,1024]{3,2,1,0:T(8,128)(2,1)} fusion(f32[64,6,4,1024,1]{3,0,2,1,4:T(8,128)S(1)} %fusion.14, bf16[1,6,6,4,4]{2,4,3,1,0:T(4,128)(2,1)S(1)} %copy-done.4), kind=kOutput, calls=%fused_computation.11 | convolution fusion | flops 454557696 | bytes 9438336 | tf_op jit(solution)/shard_map/autc,uvst->asvc/dot_general | solution.py:28
  200.2 65.7 %all-gather.9.cloned.1.call-done = bf16[1,1024,6,1024]{3,1,2,0:T(8,128)(2,1)} async-done(((bf16[1,64,6,1024]{3,1,2,0:T(8,128)(2,1)}), bf16[1,1024,6,1024]{3,1,2,0:T(8,128)(2,1)}) %all-gather.9.cloned.1.call-update) | async-done | bytes 12582928 | tf_op jit(solution)/shard_map/all_gather | solution.py:34
  265.9 12.8 %fusion.24 = f32[64,4,1024]{2,0,1:T(8,128)} fusion(bf16[1,1024,6,1024]{3,1,2,0:T(8,128)(2,1)} %all-gather.9.cloned.1.call-done, bf16[64,4,6,1024]{3,2,1,0:T(8,128)(2,1)} %fusion.8), kind=kOutput, calls=%fused_computation.23 | convolution fusion | flops 3221487616 | bytes 16777216 | tf_op jit(solution)/shard_map/asvc,cvy->asy/dot_general | solution.py:31
  278.7 5.8 fusion.29
  284.5 5.1 convolution_bitcast_fusion
  291.1 111.9 %all-reduce.3.cloned.1.call-done = f32[1024,1024]{0,1:T(8,128)} async-done(((f32[1024,1024]{0,1:T(8,128)}), f32[1024,1024]{0,1:T(8,128)}) %all-reduce.3.cloned.1.call-update) | async-done | bytes 4194320 | tf_op jit(solution)/shard_map/psum | solution.py:49
  403.0 5.5 copy.59
  408.5 4.4 fusion.9
  412.9 1.9 copy-done.2
  414.9 11.7 %cholesky.223 = f32[128,128]{1,0:T(8,128)S(1)} custom-call(f32[128,128]{1,0:T(8,128)S(1)} %cholesky.580), custom_call_target="Cholesky" | custom-call | tf_op jit(solution)/shard_map/jit(cholesky)/cholesky | solution.py:50
  426.6 9.8 %custom-call.63 = f32[1,128,128]{1,2,0:T(8,128)S(1)} custom-call(f32[1,128,128]{2,1,0:T(8,128)S(1)} %get-tuple-element.76), custom_call_target="InvertDiagBlocksLowerTriangular" | custom-call | tf_op jit(solution)/shard_map/jit(cholesky)/cholesky | solution.py:50
  440.2 2.5 cholesky.255
  442.7 11.9 %cholesky.244 = f32[128,128]{1,0:T(8,128)S(1)} custom-call(f32[128,128]{1,0:T(8,128)S(1)} %cholesky.584), custom_call_target="Cholesky" | custom-call | tf_op jit(solution)/shard_map/jit(cholesky)/cholesky | solution.py:50
  456.1 9.8 %custom-call.64 = f32[1,128,128]{1,2,0:T(8,128)S(1)} custom-call(f32[1,128,128]{2,1,0:T(8,128)S(1)} %get-tuple-element.73), custom_call_target="InvertDiagBlocksLowerTriangular" | custom-call | tf_op jit(solution)/shard_map/jit(cholesky)/cholesky | solution.py:50
  467.2 2.1 convolution_subtract_fusion.1
  469.3 11.7 %cholesky.468 = f32[128,128]{1,0:T(8,128)S(1)} custom-call(f32[128,128]{1,0:T(8,128)S(1)} %cholesky.589), custom_call_target="Cholesky" | custom-call | tf_op jit(solution)/shard_map/jit(cholesky)/cholesky | solution.py:50
  482.3 9.8 %custom-call.65 = f32[1,128,128]{1,2,0:T(8,128)S(1)} custom-call(f32[1,128,128]{2,1,0:T(8,128)S(1)} %get-tuple-element.70), custom_call_target="InvertDiagBlocksLowerTriangular" | custom-call | tf_op jit(solution)/shard_map/jit(cholesky)/cholesky | solution.py:50
  493.3 2.3 convolution_subtract_fusion.2
  495.6 12.1 %cholesky.487 = f32[128,128]{1,0:T(8,128)S(1)} custom-call(f32[128,128]{1,0:T(8,128)S(1)} %cholesky.594), custom_call_target="Cholesky" | custom-call | tf_op jit(solution)/shard_map/jit(cholesky)/cholesky | solution.py:50
  509.0 9.8 %custom-call.66 = f32[1,128,128]{1,2,0:T(8,128)S(1)} custom-call(f32[1,128,128]{2,1,0:T(8,128)S(1)} %get-tuple-element.67), custom_call_target="InvertDiagBlocksLowerTriangular" | custom-call | tf_op jit(solution)/shard_map/jit(cholesky)/cholesky | solution.py:50
  520.0 2.3 convolution_subtract_fusion.3
  522.3 11.7 %cholesky.506 = f32[128,128]{1,0:T(8,128)S(1)} custom-call(f32[128,128]{1,0:T(8,128)S(1)} %cholesky.599), custom_call_target="Cholesky" | custom-call | tf_op jit(solution)/shard_map/jit(cholesky)/cholesky | solution.py:50
  535.4 10.0 %custom-call.67 = f32[1,128,128]{1,2,0:T(8,128)S(1)} custom-call(f32[1,128,128]{2,1,0:T(8,128)S(1)} %get-tuple-element.64), custom_call_target="InvertDiagBlocksLowerTriangular" | custom-call | tf_op jit(solution)/shard_map/jit(cholesky)/cholesky | solution.py:50
  546.4 2.3 convolution_subtract_fusion.4
  548.7 11.7 %cholesky.526 = f32[128,128]{1,0:T(8,128)S(1)} custom-call(f32[128,128]{1,0:T(8,128)S(1)} %cholesky.604), custom_call_target="Cholesky" | custom-call | tf_op jit(solution)/shard_map/jit(cholesky)/cholesky | solution.py:50
  561.7 9.8 %custom-call.68 = f32[1,128,128]{1,2,0:T(8,128)S(1)} custom-call(f32[1,128,128]{2,1,0:T(8,128)S(1)} %get-tuple-element.61), custom_call_target="InvertDiagBlocksLowerTriangular" | custom-call | tf_op jit(solution)/shard_map/jit(cholesky)/cholesky | solution.py:50
  572.4 2.0 convolution_subtract_fusion.11
  574.5 11.9 %cholesky.546 = f32[128,128]{1,0:T(8,128)S(1)} custom-call(f32[128,128]{1,0:T(8,128)S(1)} %cholesky.609), custom_call_target="Cholesky" | custom-call | tf_op jit(solution)/shard_map/jit(cholesky)/cholesky | solution.py:50
  587.6 9.8 %custom-call.69 = f32[1,128,128]{1,2,0:T(8,128)S(1)} custom-call(f32[1,128,128]{2,1,0:T(8,128)S(1)} %get-tuple-element.58), custom_call_target="InvertDiagBlocksLowerTriangular" | custom-call | tf_op jit(solution)/shard_map/jit(cholesky)/cholesky | solution.py:50
  600.1 11.7 %cholesky.564 = f32[128,128]{1,0:T(8,128)S(1)} custom-call(f32[128,128]{1,0:T(8,128)S(1)} %convolution_subtract_fusion.13), custom_call_target="Cholesky" | custom-call | tf_op jit(solution)/shard_map/jit(cholesky)/cholesky | solution.py:50
  618.8 6.6 fusion.10
  625.3 27.4 %while.1 = (s32[]{:T(128)}, f32[1024,1024]{1,0:T(8,128)}, s32[8,2]{0,1:T(2,128)S(1)}, f32[8,128,128]{2,1,0:T(8,128)}, s32[]{:T(128)}) while((s32[]{:T(128)}, f32[1024,1024]{1,0:T(8,128)}, s32[8,2]{0,1:T(2,128)S(1)}, f32[8,128,128]{2,1,0:T(8,128)}, s32[]{:T(128)}) %tuple.65), condition=%wide.while_cond, body=%wide.while_body.sunk | while | flops 2 | bytes 132705 | solution.py:51
  625.9 2.8 bitcast_dynamic-update-slice_fusion.2
  629.4 2.8 bitcast_dynamic-update-slice_fusion.2
  632.8 2.8 bitcast_dynamic-update-slice_fusion.2
  636.2 2.8 bitcast_dynamic-update-slice_fusion.2
  639.6 2.8 bitcast_dynamic-update-slice_fusion.2
  643.1 2.8 bitcast_dynamic-update-slice_fusion.2
  646.5 2.8 bitcast_dynamic-update-slice_fusion.2
  649.9 2.8 bitcast_dynamic-update-slice_fusion.2
  652.7 79.6 %custom-call.70 = f32[8,128,128]{1,2,0:T(8,128)S(1)} custom-call(f32[8,128,128]{2,1,0:T(8,128)} %get-tuple-element.9), custom_call_target="InvertDiagBlocksLowerTriangular" | custom-call | tf_op jit(solution)/shard_map/jit(_solve_triangular)/triangular_solve | solution.py:51
  (95 shorter events, 47.1 us)
Async XLA Ops:
  7.2 271.5 %copy-start = (bf16[1,1024,1024]{2,1,0:T(8,128)(2,1)S(1)}, bf16[1,1024,1024]{2,1,0:T(8,128)(2,1)}, u32[]{:S(2)}) copy-start(bf16[1,1024,1024]{2,1,0:T(8,128)(2,1)} %param.13) | copy-start | bytes 6291460
  7.2 82.9 %all-gather.7.cloned.1.call-start = ((), (), s32[]{:S(2)}) async-start(), calls=%async_computation.1 | async-start | bytes 8912896 | tf_op jit(solution)/shard_map/all_gather | solution.py:22
  7.9 160.7 %all-gather.11.cloned.1.call-start = ((), (), s32[]{:S(2)}) async-start(), calls=%async_computation.3 | async-start | bytes 8912896 | tf_op jit(solution)/shard_map/all_gather | solution.py:37
  10.2 255.6 %all-gather.9.cloned.1.call-start = ((), (), s32[]{:S(2)}) async-start(), calls=%async_computation.2 | async-start | bytes 13369344 | tf_op jit(solution)/shard_map/all_gather | solution.py:34
  11.0 392.0 %all-reduce.3.cloned.1.call-start = ((), (), s32[]{:S(2)}) async-start(), calls=%async_computation | async-start | bytes 8388608 | tf_op jit(solution)/shard_map/psum | solution.py:49
  11.0 171.3 %collective-permute-start = (bf16[64,6,1024]{2,0,1:T(8,128)(2,1)}, bf16[64,6,1024]{2,0,1:T(8,128)(2,1)S(1)}, u32[]{:S(2)}, u32[]{:S(2)}) collective-permute-start(bf16[64,6,1024]{2,0,1:T(8,128)(2,1)} %bitcast.185), channel_id=1, source_target_pairs={{240,0},{0,16},{16,32},{32,48},{48,64},{64,80},{80,96},{96,112},{1... | collective-permute-start | bytes 2359304 | tf_op jit(solution)/shard_map/ppermute | solution.py:14
  14.1 264.6 %collective-permute-start.1 = (bf16[1024,1024]{1,0:T(8,128)(2,1)}, bf16[1024,1024]{1,0:T(8,128)(2,1)}, u32[]{:S(2)}, u32[]{:S(2)}) collective-permute-start(bf16[1024,1024]{1,0:T(8,128)(2,1)} %bitcast.184), channel_id=1, source_target_pairs={{240,0},{0,16},{16,32},{32,48},{48,64},{64,80},{80,96},{96,112},{1... | collective-permute-start | bytes 6291464 | tf_op jit(solution)/shard_map/ppermute | solution.py:14
  182.3 6.3 copy-start.4
  412.9 1.9 copy-start.2
  732.3 8.1 %copy-start.3 = (f32[8,128,128]{1,2,0:T(8,128)}, f32[8,128,128]{1,2,0:T(8,128)S(1)}, u32[]{:S(2)}) copy-start(f32[8,128,128]{1,2,0:T(8,128)S(1)} %custom-call.70) | copy-start | bytes 1572868
  740.8 9.1 %copy-start.1 = (bf16[1,1024,1024]{2,1,0:T(8,128)(2,1)S(1)}, bf16[1,1024,1024]{2,1,0:T(8,128)(2,1)}, u32[]{:S(2)}) copy-start(bf16[1,1024,1024]{2,1,0:T(8,128)(2,1)} %param.13) | copy-start | bytes 6291460
Sparse Core Ops, SparseCore 0:
  10.4 79.5 all-gather.6
  93.0 75.4 all-gather.10
  171.1 94.7 all-gather.8
  289.8 113.1 all-reduce.2
where the time goes:
time: 764 us; the launch traced here: 757 us
  waiting for transfers between devices  320 us (42%)
  other arithmetic  264 us (35%)
  matrix products  78.2 us (10%)
  local copies, waits for them, and re-layouts  71.6 us (9%)
  between operations  19.4 us (3%)
    another operation x30, other arithmetic, shards(): triangle = jnp.linalg.cholesky(correlation)  172 us
    psum x1, waiting for transfers between devices, shards(): correlation = lax.psum(local_correlation, 'bond')  112 us
    another operation x3, other arithmetic, shards(): solved = jax.scipy.linalg.solve_triangular(triangle, target.T, lower=True)  86.2 us
    all_gather x1, waiting for transfers between devices, shards(): current = lax.all_gather(cur_site[0], 'bond', axis=0, tiled=True)  75.9 us
    all_gather x1, waiting for transfers between devices, shards(): lax.all_gather(right_env[0], 'bond', axis=0, tiled=True)  65.7 us
    all_gather x1, waiting for transfers between devices, shards(): previous = lax.all_gather(prev_site[0], 'bond', axis=2, tiled=True)  64.7 us
    another operation x24, local copies, waits for them, and re-layouts  27.4 us
    another operation x14, matrix products, shards(): triangle = jnp.linalg.cholesky(correlation)  22.7 us
  transfers between devices with their start and end apart: 6, of which 4 were waited for; matrix products, arithmetic and copies ran while one was open for 8% of the time, Pallas kernels for 0%

commit v1 on v0

--- a/solution.py
+++ b/solution.py
@@ -3,6 +3,7 @@
 import jax.numpy as jnp
 from jax import lax
 from jax.sharding import PartitionSpec as P
+from jax.lax import all_to_all, axis_size
 
 PHYS = 4
 MPOB = 6
@@ -28,10 +29,19 @@
     mixture = jnp.einsum(
         "autc,uvst->asvc", projected, coupling, precision=lax.Precision.HIGHEST
     ).astype(jnp.bfloat16)
+
+    def _fix_bars(group_axis, k_dim, w_in):
+        return jnp.concatenate(
+            all_to_all(
+                jnp.stack([w_in for _ in range(axis_size(group_axis))], 0), group_axis, 0, 0
+            ),
+            k_dim,
+        )
+
     applied = jnp.einsum(
         "asvc,cvy->asy",
         mixture,
-        lax.all_gather(right_env[0], "bond", axis=0, tiled=True),
+        _fix_bars("bond", k_dim=0, w_in=right_env[0]),
         preferred_element_type=jnp.float32,
     )
     previous = lax.all_gather(prev_site[0], "bond", axis=2, tiled=True)

time: 764 us -> 893 us (1.17)
  waiting for transfers between devices: 320 us -> 419 us
  local copies, waits for them, and re-layouts: 71.6 us -> 94 us
    all_to_all x0 -> x1, waiting for transfers between devices: none -> 217 us  [_fix_bars(): all_to_all(jnp.stack([w_in for _ in range(axis_size(group_axis))], 0), gr...]
    all_gather x1 -> x0, waiting for transfers between devices: 65.7 us -> none  [shards(): lax.all_gather(right_env[0], 'bond', axis=0, tiled=True)]
    all_gather x1, waiting for transfers between devices: 75.9 us -> 17.1 us  [shards(): current = lax.all_gather(cur_site[0], 'bond', axis=0, tiled=True)]
    all_gather x1, waiting for transfers between devices: 64.7 us -> 75.5 us  [shards(): previous = lax.all_gather(prev_site[0], 'bond', axis=2, tiled=True)]
    all_to_all x0 -> x1, local copies, waits for them, and re-layouts: none -> 10.8 us  [_fix_bars(): all_to_all(jnp.stack([w_in for _ in range(axis_size(group_axis))], 0), gr...]
    another operation x24 -> x25, local copies, waits for them, and re-layouts: 27.4 us -> 35.7 us
  transfers between devices with their start and end apart: 6 -> 6, of which waited for: 4 -> 4; matrix products, arithmetic and copies ran while one was open for 8% -> 9% of each run, Pallas kernels for 0% -> 0%
where the time goes in v1:
time: 893 us; the launch traced here: 882 us
  waiting for transfers between devices  419 us (47%)
  other arithmetic  265 us (30%)
  local copies, waits for them, and re-layouts  94 us (11%)
  matrix products  73.9 us (8%)
  between operations  19.4 us (2%)
  starting transfers between devices  10.4 us (1%)
    all_to_all x1, waiting for transfers between devices, _fix_bars(): all_to_all(jnp.stack([w_in for _ in range(axis_size(group_axis))], 0), gr...  217 us
    another operation x30, other arithmetic, shards(): triangle = jnp.linalg.cholesky(correlation)  173 us
    psum x1, waiting for transfers between devices, shards(): correlation = lax.psum(local_correlation, 'bond')  109 us
    another operation x3, other arithmetic, shards(): solved = jax.scipy.linalg.solve_triangular(triangle, target.T, lower=True)  86.9 us
    all_gather x1, waiting for transfers between devices, shards(): previous = lax.all_gather(prev_site[0], 'bond', axis=2, tiled=True)  75.5 us
    another operation x24, local copies, waits for them, and re-layouts  28.3 us
    another operation x14, matrix products, shards(): triangle = jnp.linalg.cholesky(correlation)  22.8 us
  transfers between devices with their start and end apart: 6, of which 4 were waited for; matrix products, arithmetic and copies ran while one was open for 9% of the time, Pallas kernels for 0%

profile of v1, /device:TPU:1, one launch (start us, length us, event | category | flops | bytes accessed | tf_op | source)
XLA Modules:
  0.0 881.8 jit_solution(12693982879315769508)
XLA Ops:
  8.0 2.2 copy.58
  10.2 7.3 stack.3
  17.6 7.8 all-to-all-start
  25.4 2.5 collective-permute-start
  27.9 216.8 %all-to-all-done = bf16[16,64,6,1024]{3,1,2,0:T(8,128)(2,1)} async-done(((bf16[16,64,6,1024]{3,1,2,0:T(8,128)(2,1)}), bf16[16,64,6,1024]{3,1,2,0:T(8,128)(2,1)}, u32[]{:S(2)}, u32[]{:S(2)}) %all-to-all-start) | async-done | bytes 12582944 | tf_op jit(solution)/shard_map/all_to_all | solution.py:35
  244.7 10.8 %copy.56 = bf16[16,64,6,1024]{3,1,0,2:T(8,128)(2,1)} copy(bf16[16,64,6,1024]{3,1,2,0:T(8,128)(2,1)} %all-to-all-done) | data formatting | bytes 25165824 | tf_op jit(solution)/shard_map/all_to_all | solution.py:35
  255.5 17.1 %all-gather.5.cloned.1.call-done = bf16[1,1024,4,1024]{3,2,0,1:T(4,128)(2,1)} async-done(((bf16[1,64,4,1024]{3,2,0,1:T(4,128)(2,1)}), bf16[1,1024,4,1024]{3,2,0,1:T(4,128)(2,1)}) %all-gather.5.cloned.1.call-update) | async-done | bytes 8388624 | tf_op jit(solution)/shard_map/all_gather | solution.py:23
  272.5 13.8 %copy.84 = bf16[1,1024,4,1024]{1,3,2,0:T(8,128)(2,1)} copy(bf16[1,1024,4,1024]{3,2,0,1:T(4,128)(2,1)} %all-gather.5.cloned.1.call-done) | data formatting | bytes 16777216 | tf_op jit(solution)/shard_map/reshape | solution.py:26
  286.3 75.5 %all-gather.7.cloned.1.call-done = bf16[1,1024,4,1024]{1,2,0,3:T(4,128)(2,1)} async-done(((bf16[1,1024,4,64]{1,2,0,3:T(4,128)(2,1)}), bf16[1,1024,4,1024]{1,2,0,3:T(4,128)(2,1)}) %all-gather.7.cloned.1.call-update) | async-done | bytes 8388624 | tf_op jit(solution)/shard_map/all_gather | solution.py:47
  361.9 13.7 %copy.59 = bf16[1,1024,4,1024]{3,1,2,0:T(8,128)(2,1)} copy(bf16[1,1024,4,1024]{1,2,0,3:T(4,128)(2,1)} %all-gather.7.cloned.1.call-done) | data formatting | bytes 16777216 | tf_op jit(solution)/shard_map/all_gather | solution.py:47
  375.6 6.1 fusion.13
  381.7 9.4 %fusion.6 = bf16[64,4,6,1024]{3,2,1,0:T(8,128)(2,1)S(1)} fusion(f32[64,6,4,1024,1]{3,0,2,1,4:T(8,128)S(1)} %fusion.13, bf16[1,6,6,4,4]{2,4,3,1,0:T(4,128)(2,1)S(1)} %copy-done.4), kind=kOutput, calls=%fused_computation.9 | convolution fusion | flops 454557696 | bytes 9438336 | tf_op jit(solution)/shard_map/autc,uvst->asvc/dot_general | solution.py:29
  391.1 9.7 %fusion.24 = f32[64,4,1024]{2,0,1:T(8,128)} fusion(bf16[1024,6,1024,1]{2,0,1,3:T(8,128)(2,1)} %bitcast.172, bf16[64,4,6,1024]{3,2,1,0:T(8,128)(2,1)S(1)} %fusion.6), kind=kOutput, calls=%fused_computation.23 | convolution fusion | flops 3221487616 | bytes 16777216 | tf_op jit(solution)/shard_map/asvc,cvy->asy/dot_general | solution.py:41
  400.8 5.9 fusion.18
  406.7 5.4 convolution_bitcast_fusion
  416.6 108.7 %all-reduce.3.cloned.1.call-done = f32[1024,1024]{0,1:T(8,128)} async-done(((f32[1024,1024]{0,1:T(8,128)}), f32[1024,1024]{0,1:T(8,128)}) %all-reduce.3.cloned.1.call-update) | async-done | bytes 4194320 | tf_op jit(solution)/shard_map/psum | solution.py:59
  525.4 5.4 copy.61
  530.8 4.4 fusion.7
  537.3 11.7 %cholesky.223 = f32[128,128]{1,0:T(8,128)S(1)} custom-call(f32[128,128]{1,0:T(8,128)S(1)} %cholesky.580), custom_call_target="Cholesky" | custom-call | tf_op jit(solution)/shard_map/jit(cholesky)/cholesky | solution.py:60
  549.0 9.8 %custom-call.63 = f32[1,128,128]{1,2,0:T(8,128)S(1)} custom-call(f32[1,128,128]{2,1,0:T(8,128)S(1)} %get-tuple-element.76), custom_call_target="InvertDiagBlocksLowerTriangular" | custom-call | tf_op jit(solution)/shard_map/jit(cholesky)/cholesky | solution.py:60
  562.6 12.1 %cholesky.244 = f32[128,128]{1,0:T(8,128)S(1)} custom-call(f32[128,128]{1,0:T(8,128)S(1)} %cholesky.584), custom_call_target="Cholesky" | custom-call | tf_op jit(solution)/shard_map/jit(cholesky)/cholesky | solution.py:60
  574.7 2.5 cholesky.255
  578.7 9.8 %custom-call.64 = f32[1,128,128]{1,2,0:T(8,128)S(1)} custom-call(f32[1,128,128]{2,1,0:T(8,128)S(1)} %get-tuple-element.73), custom_call_target="InvertDiagBlocksLowerTriangular" | custom-call | tf_op jit(solution)/shard_map/jit(cholesky)/cholesky | solution.py:60
  591.9 11.7 %cholesky.468 = f32[128,128]{1,0:T(8,128)S(1)} custom-call(f32[128,128]{1,0:T(8,128)S(1)} %cholesky.589), custom_call_target="Cholesky" | custom-call | tf_op jit(solution)/shard_map/jit(cholesky)/cholesky | solution.py:60
  604.2 9.8 %custom-call.65 = f32[1,128,128]{1,2,0:T(8,128)S(1)} custom-call(f32[1,128,128]{2,1,0:T(8,128)S(1)} %get-tuple-element.70), custom_call_target="InvertDiagBlocksLowerTriangular" | custom-call | tf_op jit(solution)/shard_map/jit(cholesky)/cholesky | solution.py:60
  615.2 2.3 convolution_subtract_fusion.2
  617.6 11.9 %cholesky.487 = f32[128,128]{1,0:T(8,128)S(1)} custom-call(f32[128,128]{1,0:T(8,128)S(1)} %cholesky.594), custom_call_target="Cholesky" | custom-call | tf_op jit(solution)/shard_map/jit(cholesky)/cholesky | solution.py:60
  630.1 9.8 %custom-call.66 = f32[1,128,128]{1,2,0:T(8,128)S(1)} custom-call(f32[1,128,128]{2,1,0:T(8,128)S(1)} %get-tuple-element.67), custom_call_target="InvertDiagBlocksLowerTriangular" | custom-call | tf_op jit(solution)/shard_map/jit(cholesky)/cholesky | solution.py:60
  641.0 2.3 convolution_subtract_fusion.3
  643.4 11.7 %cholesky.506 = f32[128,128]{1,0:T(8,128)S(1)} custom-call(f32[128,128]{1,0:T(8,128)S(1)} %cholesky.599), custom_call_target="Cholesky" | custom-call | tf_op jit(solution)/shard_map/jit(cholesky)/cholesky | solution.py:60
  655.7 10.0 %custom-call.67 = f32[1,128,128]{1,2,0:T(8,128)S(1)} custom-call(f32[1,128,128]{2,1,0:T(8,128)S(1)} %get-tuple-element.64), custom_call_target="InvertDiagBlocksLowerTriangular" | custom-call | tf_op jit(solution)/shard_map/jit(cholesky)/cholesky | solution.py:60
  666.8 2.3 convolution_subtract_fusion.4
  669.1 11.7 %cholesky.526 = f32[128,128]{1,0:T(8,128)S(1)} custom-call(f32[128,128]{1,0:T(8,128)S(1)} %cholesky.604), custom_call_target="Cholesky" | custom-call | tf_op jit(solution)/shard_map/jit(cholesky)/cholesky | solution.py:60
  681.4 9.8 %custom-call.68 = f32[1,128,128]{1,2,0:T(8,128)S(1)} custom-call(f32[1,128,128]{2,1,0:T(8,128)S(1)} %get-tuple-element.61), custom_call_target="InvertDiagBlocksLowerTriangular" | custom-call | tf_op jit(solution)/shard_map/jit(cholesky)/cholesky | solution.py:60
  694.3 12.1 %cholesky.546 = f32[128,128]{1,0:T(8,128)S(1)} custom-call(f32[128,128]{1,0:T(8,128)S(1)} %cholesky.609), custom_call_target="Cholesky" | custom-call | tf_op jit(solution)/shard_map/jit(cholesky)/cholesky | solution.py:60
  707.0 9.8 %custom-call.69 = f32[1,128,128]{1,2,0:T(8,128)S(1)} custom-call(f32[1,128,128]{2,1,0:T(8,128)S(1)} %get-tuple-element.58), custom_call_target="InvertDiagBlocksLowerTriangular" | custom-call | tf_op jit(solution)/shard_map/jit(cholesky)/cholesky | solution.py:60
  719.5 11.7 %cholesky.564 = f32[128,128]{1,0:T(8,128)S(1)} custom-call(f32[128,128]{1,0:T(8,128)S(1)} %convolution_subtract_fusion.13), custom_call_target="Cholesky" | custom-call | tf_op jit(solution)/shard_map/jit(cholesky)/cholesky | solution.py:60
  741.6 6.7 fusion.8
  748.3 28.4 %while.1 = (s32[]{:T(128)}, f32[1024,1024]{1,0:T(8,128)}, s32[8,2]{0,1:T(2,128)S(1)}, f32[8,128,128]{2,1,0:T(8,128)}, s32[]{:T(128)}) while((s32[]{:T(128)}, f32[1024,1024]{1,0:T(8,128)}, s32[8,2]{0,1:T(2,128)S(1)}, f32[8,128,128]{2,1,0:T(8,128)}, s32[]{:T(128)}) %tuple.65), condition=%wide.while_cond, body=%wide.while_body.sunk | while | flops 2 | bytes 132205 | solution.py:61
  749.0 2.9 bitcast_dynamic-update-slice_fusion.2
  752.5 2.9 bitcast_dynamic-update-slice_fusion.2
  756.1 2.9 bitcast_dynamic-update-slice_fusion.2
  759.6 2.9 bitcast_dynamic-update-slice_fusion.2
  763.2 2.9 bitcast_dynamic-update-slice_fusion.2
  766.7 2.9 bitcast_dynamic-update-slice_fusion.2
  770.3 2.9 bitcast_dynamic-update-slice_fusion.2
  773.8 2.8 bitcast_dynamic-update-slice_fusion.2
  776.7 80.2 %custom-call.70 = f32[8,128,128]{1,2,0:T(8,128)} custom-call(f32[8,128,128]{2,1,0:T(8,128)} %get-tuple-element.9), custom_call_target="InvertDiagBlocksLowerTriangular" | custom-call | tf_op jit(solution)/shard_map/jit(_solve_triangular)/triangular_solve | solution.py:61
  (98 shorter events, 57.1 us)
Async XLA Ops:
  7.2 393.6 %copy-start = (bf16[1,1024,1024]{2,1,0:T(8,128)(2,1)S(1)}, bf16[1,1024,1024]{2,1,0:T(8,128)(2,1)}, u32[]{:S(2)}) copy-start(bf16[1,1024,1024]{2,1,0:T(8,128)(2,1)} %param.13) | copy-start | bytes 6291460
  7.2 265.4 %all-gather.5.cloned.1.call-start = ((), (), s32[]{:S(2)}) async-start(), calls=%async_computation.2 | async-start | bytes 8912896 | tf_op jit(solution)/shard_map/all_gather | solution.py:23
  7.9 353.9 %all-gather.7.cloned.1.call-start = ((), (), s32[]{:S(2)}) async-start(), calls=%async_computation.3 | async-start | bytes 8912896 | tf_op jit(solution)/shard_map/all_gather | solution.py:47
  17.6 7.8 copy-start.5
  17.6 227.1 %all-to-all-start = ((bf16[16,64,6,1024]{3,1,2,0:T(8,128)(2,1)}), bf16[16,64,6,1024]{3,1,2,0:T(8,128)(2,1)}, u32[]{:S(2)}, u32[]{:S(2)}) async-start(bf16[16,64,6,1024]{3,1,2,0:T(8,128)(2,1)} %stack.3), calls=%async_computation | async-start | bytes 25165824 | tf_op jit(solution)/shard_map/all_to_all | solution.py:35
  25.3 500.0 %all-reduce.3.cloned.1.call-start = ((), (), s32[]{:S(2)}) async-start(), calls=%async_computation.1 | async-start | bytes 8388608 | tf_op jit(solution)/shard_map/psum | solution.py:59
  25.4 350.2 %collective-permute-start = (bf16[64,6,1024]{2,0,1:T(8,128)(2,1)S(1)}, bf16[64,6,1024]{2,0,1:T(8,128)(2,1)}, u32[]{:S(2)}, u32[]{:S(2)}) collective-permute-start(bf16[64,6,1024]{2,0,1:T(8,128)(2,1)S(1)} %bitcast.184), channel_id=1, source_target_pairs={{240,0},{0,16},{16,32},{32,48},{48,64},{64,80},{80,96},{96,112},{1... | collective-permute-start | bytes 2359304 | tf_op jit(solution)/shard_map/ppermute | solution.py:15
  27.9 372.9 %collective-permute-start.1 = (bf16[1024,1024]{1,0:T(8,128)(2,1)}, bf16[1024,1024]{1,0:T(8,128)(2,1)}, u32[]{:S(2)}, u32[]{:S(2)}) collective-permute-start(bf16[1024,1024]{1,0:T(8,128)(2,1)} %bitcast.183), channel_id=1, source_target_pairs={{240,0},{0,16},{16,32},{32,48},{48,64},{64,80},{80,96},{96,112},{1... | collective-permute-start | bytes 6291464 | tf_op jit(solution)/shard_map/ppermute | solution.py:15
  375.6 6.1 copy-start.4
  535.2 2.0 copy-start.1
  741.5 115.3 %copy-start.2 = (f32[256,1024]{0,1:T(8,128)S(1)}, f32[256,1024]{0,1:T(8,128)}, u32[]{:S(2)}) copy-start(f32[256,1024]{0,1:T(8,128)} %copy.70) | copy-start | bytes 3145732
  856.8 7.2 copy-start.3
Sparse Core Ops, SparseCore 0:
  10.4 262.0 all-gather.4
  275.5 86.2 all-gather.6
  412.2 113.1 all-reduce.2
